TPU v7x, 512 devices: a whole 4x4x16 slice. The times are simulated.
512 devices in a mesh: node: 128 (over z, y, core), local: 4 (over x).
Axes of the slice: x: 4, y: 4, z: 16, core: 2. Of those that a mesh axis runs over, the one named last changes fastest.
Arguments:
- table: bfloat16 [131072, 512], P(('node', 'local')), may hold values from -6 to 6
- w_in: bfloat16 [1, 512, 2048], replicated, may hold values from -0.25 to 0.25
- w_out: bfloat16 [1, 512, 512], replicated, may hold values from -0.25 to 0.25
- owner_node: int32 [131072, 1], P(('node', 'local')), may hold values from 0 to 127; in each aligned block of 256 rows (0 to 255, 256 to 511, ...) at most 3 rows name the same one
- item_row: int32 [131072], P(('node', 'local')), may hold values from 0 to 1023
- history_lengths: int32 [512, 4], P(('node', 'local')), may hold values from 1 to 128, 256 in all within a row
- cotangent: bfloat16 [131072, 512], P(('node', 'local')), may hold values from -6 to 6
Outputs:
- table_grad: bfloat16 [131072, 512], P(('node', 'local'))
Inputs may be any that keep to these rules, and one draw needn't show every extreme that they name: `owner_node`: of the 256 items of one device, at most 3 name the same node, and this many do in some device's items in every draw. `history_lengths`: each row sums to 256, and some history is 128 items long.
All inputs are finite; a program needn't handle non-finite values.
Results may differ from a plain program's by a relative error of at most 0.018.
Values may be sent and summed in bfloat16 or wider, within the bound.
No kernel may reach another device: no remote copies, remote signals or barrier semaphores. Data moves between devices by JAX's collectives and lax.ppermute only.
A program may use at most 64 MiB of HBM per device.

v0:
```python
import math

import jax
import jax.numpy as jnp
from jax import lax
from jax.sharding import PartitionSpec as P

HEADS = 4


def normalize(value):
    average = jnp.mean(value, axis=-1, keepdims=True)
    centered = value - average
    spread = jnp.mean(centered * centered, axis=-1, keepdims=True)
    return centered * lax.rsqrt(spread + 1e-05)


def history_weights(lengths, tok_rows):
    seq_ends = jnp.cumsum(lengths)
    places = jnp.arange(tok_rows, dtype=jnp.int32)
    segment = jnp.sum((places[:, None] >= seq_ends[None, :]).astype(jnp.int32), axis=1)
    member = segment[:, None] == jnp.arange(lengths.shape[0], dtype=jnp.int32)[None, :]
    own_length = jnp.sum(jnp.where(member, lengths[None, :], 0), axis=1)
    allowed = (segment[:, None] == segment[None, :]) & (places[None, :] <= places[:, None])
    factor = 1.0 / own_length.astype(jnp.float32)
    return jnp.where(allowed, factor[:, None], jnp.float32(0.0))


def one_layer(hidden, weights, layer_in, layer_out):
    tok_rows = hidden.shape[0]
    model_width = hidden.shape[1]
    head_size = model_width // HEADS
    normed = normalize(hidden).astype(jnp.bfloat16)
    projected = jax.nn.silu(jnp.dot(normed, layer_in, preferred_element_type=jnp.float32)).astype(
        jnp.bfloat16
    )
    gate_rows = projected[:, :model_width]
    value_rows = projected[:, model_width : 2 * model_width]
    query_rows = projected[:, 2 * model_width : 3 * model_width]
    key_rows = projected[:, 3 * model_width :]

    def by_head(part):
        return part.reshape(tok_rows, HEADS, head_size).transpose(1, 0, 2)

    scale = 1.0 / math.sqrt(head_size)

    def one_head(head_parts):
        query_head, key_head, value_head = head_parts
        scores = jnp.dot(query_head, key_head.T, preferred_element_type=jnp.float32) * scale
        attention = (jax.nn.silu(scores) * weights).astype(jnp.bfloat16)
        return jnp.dot(attention, value_head, preferred_element_type=jnp.float32)

    mixed_rows = lax.map(
        jax.checkpoint(one_head), (by_head(query_rows), by_head(key_rows), by_head(value_rows))
    )
    mixed_rows = mixed_rows.transpose(1, 0, 2).reshape(tok_rows, model_width)
    gated_rows = (normalize(mixed_rows) * gate_rows.astype(jnp.float32)).astype(jnp.bfloat16)
    return jnp.dot(gated_rows, layer_out, preferred_element_type=jnp.float32) + hidden


def layer_stack(embedded, weights, w_in, w_out):
    hidden = embedded.astype(jnp.float32)
    hidden = one_layer(hidden, weights, w_in[0], w_out[0])
    return hidden


def embedding_grad(embedded, lengths, cot_rows, w_in, w_out):
    weights = history_weights(lengths, embedded.shape[0])
    outputs, pullback = jax.vjp(
        lambda entries: layer_stack(entries, weights, w_in, w_out), embedded
    )
    return pullback(cot_rows.astype(outputs.dtype))[0]


def per_device(table, w_in, w_out, owner_node, item_row, history_lengths, cotangent):
    tok_rows = item_row.shape[0]
    node_count = lax.axis_size("node")
    local_index = lax.axis_index("local")
    capacity = 3 * tok_rows // (2 * node_count)
    slot_count = node_count * capacity
    rows_here = table.shape[0]
    model_width = table.shape[1]
    owner = owner_node[:, 0]
    target_hot = (owner[:, None] == jnp.arange(node_count, dtype=jnp.int32)[None, :]).astype(
        jnp.bfloat16
    )
    places = jnp.arange(tok_rows, dtype=jnp.int32)
    earlier = (places[None, :] < places[:, None]).astype(jnp.bfloat16)
    before = jnp.dot(earlier, target_hot, preferred_element_type=jnp.float32)
    slot_rank = jnp.sum(before * target_hot, axis=1).astype(jnp.int32)
    token_slot = owner * capacity + slot_rank
    sent_ids = jnp.zeros((slot_count,), jnp.int32).at[token_slot].set(item_row)
    asked_ids = lax.all_to_all(sent_ids, "node", split_axis=0, concat_axis=0, tiled=True)
    node_rows = lax.all_gather(table, "local", axis=0, tiled=True)
    answers = node_rows[asked_ids]
    arrived_rows = lax.all_to_all(answers, "node", split_axis=0, concat_axis=0, tiled=True)
    embedded = arrived_rows[token_slot]
    grads = embedding_grad(embedded, history_lengths[0], cotangent, w_in, w_out)
    grad_slots = jnp.zeros((slot_count, model_width), jnp.bfloat16).at[token_slot].set(grads)
    node_grads = lax.all_to_all(grad_slots, "node", split_axis=0, concat_axis=0, tiled=True)
    grad_rows_ids = lax.all_gather(asked_ids, "local", axis=0, tiled=True)
    all_grads = lax.all_gather(node_grads, "local", axis=0, tiled=True)
    grad_offset = grad_rows_ids - local_index * rows_here
    grad_owned = (grad_offset >= 0) & (grad_offset < rows_here)
    target_row = jnp.where(grad_owned, grad_offset, rows_here)
    row_totals = (
        jnp.zeros((rows_here + 1, model_width), jnp.float32)
        .at[target_row]
        .add(all_grads.astype(jnp.float32))[:rows_here]
    )
    return row_totals.astype(jnp.bfloat16)


def solution(mesh):
    return jax.shard_map(
        per_device,
        mesh=mesh,
        in_specs=(
            P(("node", "local"), None),
            P(),
            P(),
            P(("node", "local"), None),
            P(("node", "local")),
            P(("node", "local"), None),
            P(("node", "local"), None),
        ),
        out_specs=P(("node", "local"), None),
        check_vma=False,
    )
```

profile of v0, /device:TPU:1, one launch (start us, length us, event | category | flops | bytes accessed | tf_op | source)
XLA Modules:
  0.0 221.9 jit_solution(523215074498221670)
XLA Ops:
  7.3 1.0 fusion.66
  8.9 1.6 scatter_custom_fusion
  10.7 35.2 %all_to_all.39 = s32[128,3,1]{1,2,0:T(1,128)S(1)} all-to-all(s32[128,3,1]{1,2,0:T(1,128)S(1)} %bitcast.175), channel_id=1, replica_groups=mesh['node'=128,'local'=4] {'node'}, dimensions={0} | all-to-all | bytes 3072 | tf_op jit(solution)/shard_map/all_to_all | solution.py:93
  46.6 3.5 %gather_fusion = bf16[384,512]{1,0:T(8,128)(2,1)S(1)} fusion(bf16[1024,512]{1,0:T(8,128)(2,1)} %all-gather.4.cloned.1.call-done, s32[1024]{0:T(1024)S(1)} %pad_clamp_fusion.1), kind=kCustom, calls=%fused_computation | custom fusion | bytes 787968 | tf_op jit(solution)/shard_map/gather | solution.py:95
  50.0 1.0 all_to_all.30
  51.0 16.5 %all-to-all-start.1 = ((bf16[128,3,512]{2,1,0:T(4,128)(2,1)}), bf16[128,3,512]{2,1,0:T(4,128)(2,1)S(1)}, u32[]{:S(2)}, u32[]{:S(2)}) async-start(bf16[128,3,512]{2,1,0:T(4,128)(2,1)} %all_to_all.30), calls=%async_computation.1 | async-start | bytes 1048576 | tf_op jit(solution)/shard_map/all_to_all | solution.py:96
  68.1 30.2 %all-to-all-done.1 = bf16[128,3,512]{2,1,0:T(4,128)(2,1)S(1)} async-done(((bf16[128,3,512]{2,1,0:T(4,128)(2,1)}), bf16[128,3,512]{2,1,0:T(4,128)(2,1)S(1)}, u32[]{:S(2)}, u32[]{:S(2)}) %all-to-all-start.1) | async-done | bytes 393248 | tf_op jit(solution)/shard_map/all_to_all | solution.py:96
  98.7 1.2 gather_fusion.1
  100.2 2.5 %multiply_convert_fusion.2 = (bf16[256,2048]{1,0:T(8,128)(2,1)}, f32[256,2048]{1,0:T(8,128)}) fusion(bf16[1,512,2048]{2,1,0:T(8,128)(2,1)S(1)} %copy-done, bf16[256,512]{1,0:T(8,128)(2,1)S(1)} %gather_fusion.1, f32[256]{0:T(256)S(1)} %fusion.97, f32[256]{0:T(256)S(1)} %broadcast_multiply_fusion.1), kind=kOutput, calls=%fused_computation.70 | convolution fusion | flops 540016640 | bytes 5507072 | tf_op jit(solution)/shard_map/jvp()/dot_general | solution.py:34
  102.7 1.2 slice_bitcast_fusion
  104.7 4.9 %while.30 = (s32[]{:T(128)}, f32[4,256,128]{2,1,0:T(8,128)S(1)}, bf16[4,256,128]{2,1,0:T(8,128)(2,1)S(1)}, bf16[4,256,128]{2,1,0:T(8,128)(2,1)}, bf16[4,256,128]...) while((s32[]{:T(128)}, f32[4,256,128]{2,1,0:T(8,128)S(1)}, ...), condition=%wide.region_8.9_spmd.clone, body=%wide.region_7.8_spmd.clone.sunk | while | flops 34275328 | bytes 332893 | solution.py:53
  104.7 1.2 fusion.139
  105.9 1.2 fusion.139
  107.1 1.2 fusion.139
  108.3 1.2 fusion.139
  109.9 1.6 multiply_reduce_fusion
  111.5 1.9 fusion.102
  115.1 13.5 %while.31 = (s32[]{:T(128)}, bf16[4,256,128]{2,1,0:T(8,128)(2,1)S(1)}, bf16[4,256,128]{2,1,0:T(8,128)(2,1)}, bf16[4,256,128]{2,1,0:T(8,128)(2,1)}, bf16[4,256,12...) while((s32[]{:T(128)}, ...), condition=%wide.region_14.15_spmd.clone, body=%wide.region_13.14_spmd.clone.sunk | while | flops 85458944 | bytes 3147933 | solution.py:53
  117.6 0.9 fusion.153
  118.7 0.9 dynamic-slice_bitcast_fusion.6
  121.0 0.9 fusion.153
  124.4 0.9 fusion.153
  127.8 0.9 fusion.153
  128.7 1.0 copy_bitcast_fusion
  129.7 1.0 copy_bitcast_fusion.2
  130.7 2.8 %fusion.81 = (f32[256]{0:T(256)S(1)}, f32[256,512]{1,0:T(8,128)S(1)}) fusion(bf16[256,512]{1,0:T(8,128)(2,1)S(1)} %gather_fusion.1, f32[256]{0:T(256)S(1)} %broadcast_multiply_fusion.1, bf16[1,512,2048]{2,1,0:T(8,128)(2,1)S(1)} %copy-done, f32[256,2048]{1,0:T(8,128)} %get-tuple-element.321, bf16[256,512]{1,0:T(8,128)(2,1)} %get-tuple-element.314, ...), kind=kOutput, calls=%fused_computation.96 | convolution fusion | flops 546569984 | bytes 6031360 | tf_op jit(solution)/shard_map/transpose(jvp())/dot_general | solution.py:34
  133.8 2.0 scatter_custom_fusion.1
  136.0 39.7 %all_to_all.40 = bf16[128,3,512]{2,1,0:T(4,128)(2,1)S(1)} all-to-all(bf16[128,3,512]{2,1,0:T(4,128)(2,1)S(1)} %all_to_all.33), channel_id=1, replica_groups=mesh['node'=128,'local'=4] {'node'}, dimensions={0} | all-to-all | bytes 786432 | tf_op jit(solution)/shard_map/all_to_all | solution.py:100
  175.7 1.1 all_to_all.35
  178.3 8.3 %all-gather = s32[4,1,384]{2,1,0:T(1,128)S(1)} all-gather(s32[1,1,384]{2,1,0:T(1,128)S(1)} %reshape.200), channel_id=1, replica_groups=mesh['node'=128,'local'=4] {'local'}, dimensions={0}, use_global_device_ids=true | all-gather | bytes 7680 | tf_op jit(solution)/shard_map/all_gather | solution.py:101
  186.7 17.3 %all-gather.6.cloned.1.call-done = bf16[1536,512]{1,0:T(8,128)(2,1)} async-done(((bf16[384,512]{1,0:T(8,128)(2,1)}), bf16[1536,512]{1,0:T(8,128)(2,1)}) %all-gather.6.cloned.1.call-update) | async-done | bytes 1572880 | tf_op jit(solution)/shard_map/all_gather | solution.py:102
  204.0 10.4 %scatter_custom_fusion.2 = f32[257,512]{1,0:T(8,128)S(1)} fusion(s32[1536]{0:T(1024)S(1)} %compare_select_fusion, bf16[1536,512]{1,0:T(8,128)(2,1)} %all-gather.6.cloned.1.call-done, f32[]{:T(128)} %constant.111.clone.1), kind=kCustom, calls=%fused_computation.59 | custom fusion | flops 1572864 | bytes 2099204 | tf_op jit(solution)/shard_map/scatter-add | solution.py:109
  (88 shorter events, 18.1 us)
Async XLA Ops:
  6.5 93.7 %copy-start = (bf16[1,512,2048]{2,1,0:T(8,128)(2,1)S(1)}, bf16[1,512,2048]{2,1,0:T(8,128)(2,1)}, u32[]{:S(2)}) copy-start(bf16[1,512,2048]{2,1,0:T(8,128)(2,1)} %param.12) | copy-start | bytes 6291460
  6.5 40.0 %all-gather.4.cloned.1.call-start = ((), (), s32[]{:S(2)}) async-start(), calls=%async_computation.3 | async-start | bytes 1310720 | tf_op jit(solution)/shard_map/all_gather | solution.py:94
  8.9 59.0 %copy-start.6 = (s32[256,1]{0,1:T(1,128)}, s32[256,1]{0,1:T(1,128)S(1)}, u32[]{:S(2)}) copy-start(s32[256,1]{0,1:T(1,128)S(1)} %compare_select_fusion.2) | copy-start | bytes 3076
  45.9 0.6 copy-start.2
  46.6 21.2 %copy-start.7 = (s32[1,4]{1,0:T(1,128)S(1)}, s32[1,4]{1,0:T(1,128)}, u32[]{:S(2)}) copy-start(s32[1,4]{1,0:T(1,128)} %param.16) | copy-start | bytes 52
  51.0 47.3 %all-to-all-start.1 = ((bf16[128,3,512]{2,1,0:T(4,128)(2,1)}), bf16[128,3,512]{2,1,0:T(4,128)(2,1)S(1)}, u32[]{:S(2)}, u32[]{:S(2)}) async-start(bf16[128,3,512]{2,1,0:T(4,128)(2,1)} %all_to_all.30), calls=%async_computation.1 | async-start | bytes 1048576 | tf_op jit(solution)/shard_map/all_to_all | solution.py:96
  67.5 136.5 %all-gather.6.cloned.1.call-start = ((), (), s32[]{:S(2)}) async-start(), calls=%async_computation.4 | async-start | bytes 1966080 | tf_op jit(solution)/shard_map/all_gather | solution.py:102
  100.2 2.5 %copy-start.4 = (f32[256]{0:T(256)}, f32[256]{0:T(256)S(1)}, u32[]{:S(2)}) copy-start(f32[256]{0:T(256)S(1)} %fusion.97) | copy-start | bytes 3076
  130.7 2.8 %copy-start.5 = (f32[256]{0:T(256)S(1)}, f32[256]{0:T(256)}, u32[]{:S(2)}) copy-start(f32[256]{0:T(256)} %copy-done.4) | copy-start | bytes 3076
  130.7 3.1 %copy-start.1 = (bf16[256,512]{1,0:T(8,128)(2,1)S(1)}, bf16[256,512]{1,0:T(8,128)(2,1)}, u32[]{:S(2)}) copy-start(bf16[256,512]{1,0:T(8,128)(2,1)} %param.17) | copy-start | bytes 786436
  135.7 41.6 %copy-start.3 = (s32[128,3,1]{1,2,0:T(1,128)S(1)}, s32[128,3,1]{1,2,0:T(1,128)}, u32[]{:S(2)}) copy-start(s32[128,3,1]{1,2,0:T(1,128)} %copy-done.2) | copy-start | bytes 4612
Sparse Core Ops, SparseCore 0:
  9.5 36.0 all-gather.3
  176.9 27.0 all-gather.5
where the time goes:
time: 223 us; the launch traced here: 222 us
  blocking collectives  83.3 us (37%)
  waiting for transfers between devices  48.2 us (22%)
  matrix products  22 us (10%)
  local copies, waits for them, and re-layouts  20.1 us (9%)
  other arithmetic  17.8 us (8%)
  starting transfers between devices  16.7 us (7%)
  between operations  13.7 us (6%)
    all_to_all x1, blocking collectives, per_device(): lax.all_to_all(grad_slots, 'node', split_axis=0, concat_axis=0, tiled=True)  39.7 us
    all_to_all x1, blocking collectives, per_device(): lax.all_to_all(sent_ids, 'node', split_axis=0, concat_axis=0, tiled=True)  35.2 us
    all_to_all x1, waiting for transfers between devices, per_device(): lax.all_to_all(answers, 'node', split_axis=0, concat_axis=0, tiled=True)  30.2 us
    all_gather x1, waiting for transfers between devices, per_device(): all_grads = lax.all_gather(node_grads, 'local', axis=0, tiled=True)  17.3 us
    all_to_all x1, starting transfers between devices, per_device(): lax.all_to_all(answers, 'node', split_axis=0, concat_axis=0, tiled=True)  16.5 us
    scatter-add x1, other arithmetic, per_device(): row_totals = jnp.zeros((rows_here + 1, model_width), jnp.float32).at[targ...  10.4 us
    dot_general x12, matrix products, one_head(): return jnp.dot(attention, value_head, preferred_element_type=jnp.float32)  9.24 us
    all_gather x1, blocking collectives, per_device(): grad_rows_ids = lax.all_gather(asked_ids, 'local', axis=0, tiled=True)  8.3 us
  transfers between devices with their start and end apart: 3, of which 2 were waited for; matrix products, arithmetic and copies ran while one was open for 2% of the time, Pallas kernels for 0%

commit v1 on v0

v1 whole, which is shorter than its diff:
```python
import math

import jax
import jax.numpy as jnp
from jax import lax
from jax.experimental import pallas as pl
from jax.experimental.pallas import tpu as pltpu
from jax.sharding import PartitionSpec as P

HEADS = 4
CAP = 3
LANES = 128
F32 = jnp.float32
BF16 = jnp.bfloat16
VMEM = pl.BlockSpec(memory_space=pltpu.VMEM)
SMEM = pl.BlockSpec(memory_space=pltpu.SMEM)


def dot(a, b, ca=1, cb=0):
    return lax.dot_general(a, b, (((ca,), (cb,)), ((), ())), preferred_element_type=F32)


def ranked(owner, nodes):
    count = owner.shape[0]
    hot = owner == lax.broadcasted_iota(jnp.int32, (count, nodes), 1)
    hot = jnp.where(hot, 1.0, 0.0)
    row = lax.broadcasted_iota(jnp.int32, (count, count), 0)
    col = lax.broadcasted_iota(jnp.int32, (count, count), 1)
    earlier = jnp.where(col < row, 1.0, 0.0).astype(BF16)
    before = dot(earlier, hot.astype(BF16))
    rank = jnp.sum(before * hot, axis=1, keepdims=True)
    return hot, rank


def ask_kernel(owner_ref, row_ref, ids_ref):
    nodes = ids_ref.shape[0]
    count = owner_ref.shape[0]
    hot, rank = ranked(owner_ref[...], nodes)
    rows = row_ref[...]
    place = lax.broadcasted_iota(jnp.int32, (count, LANES), 1) == rank.astype(jnp.int32)
    high = jnp.where(place, (rows >> 5).astype(F32), 0.0).astype(BF16)
    low = jnp.where(place, (rows & 31).astype(F32), 0.0).astype(BF16)
    hot = hot.astype(BF16)
    ids = dot(hot, high, 0, 0) * 32.0 + dot(hot, low, 0, 0)
    ids_ref[...] = ids.astype(jnp.int32)


def answer_kernel(ids_ref, table_ref, out_ref, wide_ref):
    nodes = ids_ref.shape[0]
    rows, width = table_ref.shape
    pieces = width // LANES
    ids = ids_ref[...]
    table = table_ref[...]
    place = lax.broadcasted_iota(jnp.int32, (nodes, rows), 1)
    for slot in range(CAP):
        hot = jnp.where(ids[:, slot : slot + 1] == place, 1.0, 0.0).astype(BF16)
        picked = dot(hot, table)
        for piece in range(pieces):
            wide_ref[pl.ds(slot * pieces + piece, nodes, stride=CAP * pieces), :] = picked[
                :, piece * LANES : (piece + 1) * LANES
            ]
    out_ref[...] = wide_ref[...].astype(BF16)


def unpack(message_ref, wide_ref, nodes, pieces):
    wide_ref[...] = message_ref[...].astype(F32)
    slots = []
    for slot in range(CAP):
        parts = [
            wide_ref[pl.ds(slot * pieces + piece, nodes, stride=CAP * pieces), :].astype(BF16)
            for piece in range(pieces)
        ]
        slots.append(jnp.concatenate(parts, axis=1))
    return slots


def centre(value):
    average = jnp.mean(value, axis=1, keepdims=True)
    centered = value - average
    spread = jnp.mean(centered * centered, axis=1, keepdims=True)
    inverse = lax.rsqrt(spread + 1e-05)
    return centered * inverse, inverse


def centre_back(normed, inverse, cot):
    return inverse * (
        cot
        - jnp.mean(cot, axis=1, keepdims=True)
        - normed * jnp.mean(cot * normed, axis=1, keepdims=True)
    )


def gated(value):
    gate = 0.5 + 0.5 * jnp.tanh(0.5 * value)
    kept = value * gate
    return kept, gate + kept * (1.0 - gate)


def layer_kernel(lengths_ref, owner_ref, message_ref, cot_ref, w_in_ref, w_out_ref, out_ref, wide_ref):
    tokens, width = cot_ref.shape
    head = width // HEADS
    pieces = width // LANES
    nodes = message_ref.shape[0] // (CAP * pieces)
    hot, rank = ranked(owner_ref[...], nodes)
    picks = [jnp.where(rank == float(slot), hot, 0.0).astype(BF16) for slot in range(CAP)]
    arrived = unpack(message_ref, wide_ref, nodes, pieces)
    embedded = dot(jnp.concatenate(picks, axis=1), jnp.concatenate(arrived, axis=0))

    row = lax.broadcasted_iota(jnp.int32, (tokens, 1), 0)
    col = lax.broadcasted_iota(jnp.int32, (1, tokens), 1)
    seqs = lengths_ref.shape[1]
    row_seg, col_seg, end = jnp.zeros_like(row), jnp.zeros_like(col), jnp.int32(0)
    own = jnp.full((tokens, 1), lengths_ref[0, 0], jnp.int32)
    for seq in range(seqs - 1):
        end = end + lengths_ref[0, seq]
        row_seg = row_seg + (row >= end).astype(jnp.int32)
        col_seg = col_seg + (col >= end).astype(jnp.int32)
        own = jnp.where(row >= end, lengths_ref[0, seq + 1], own)
    factor = 1.0 / own.astype(F32)
    weights = jnp.where((row_seg == col_seg) & (col <= row), factor, 0.0)

    normed, inverse = centre(embedded)
    normed_low = normed.astype(BF16)
    parts, slopes = [], []
    for part in range(4):
        kept, slope = gated(dot(normed_low, w_in_ref[:, part * width : (part + 1) * width]))
        parts.append(kept.astype(BF16))
        slopes.append(slope)
    gate_rows, value_rows, query_rows, key_rows = parts
    scale = 1.0 / math.sqrt(head)
    attentions, score_slopes, mixed = [], [], []
    for e in range(HEADS):
        cols = slice(e * head, (e + 1) * head)
        kept, slope = gated(dot(query_rows[:, cols], key_rows[:, cols], 1, 1) * scale)
        attention = (kept * weights).astype(BF16)
        attentions.append(attention)
        score_slopes.append(slope * (weights * scale))
        mixed.append(dot(attention, value_rows[:, cols]))
    mixed_normed, mixed_inverse = centre(jnp.concatenate(mixed, axis=1))

    cot = cot_ref[...]
    gated_cot = dot(cot, w_out_ref[...], 1, 1).astype(BF16).astype(F32)
    gate_cot = gated_cot * mixed_normed
    mixed_cot = centre_back(mixed_normed, mixed_inverse, gated_cot * gate_rows.astype(F32)).astype(BF16)
    value_cots, query_cots, key_cots = [], [], []
    for e in range(HEADS):
        cols = slice(e * head, (e + 1) * head)
        head_cot = mixed_cot[:, cols]
        value_cots.append(dot(attentions[e], head_cot, 0, 0))
        score_cot = (dot(head_cot, value_rows[:, cols], 1, 1) * score_slopes[e]).astype(BF16)
        query_cots.append(dot(score_cot, key_rows[:, cols]))
        key_cots.append(dot(score_cot, query_rows[:, cols], 0, 0))
    normed_cot = jnp.zeros((tokens, width), F32)
    for part, part_cot in enumerate([[gate_cot], value_cots, query_cots, key_cots]):
        whole = part_cot[0] if len(part_cot) == 1 else jnp.concatenate(part_cot, axis=1)
        whole = (whole.astype(BF16).astype(F32) * slopes[part]).astype(BF16)
        normed_cot = normed_cot + dot(whole, w_in_ref[:, part * width : (part + 1) * width], 1, 1)
    grads = cot.astype(F32) + centre_back(normed, inverse, normed_cot.astype(BF16).astype(F32))
    grads = grads.astype(BF16)
    for slot in range(CAP):
        placed = dot(picks[slot], grads, 0, 0)
        for piece in range(pieces):
            wide_ref[pl.ds(slot * pieces + piece, nodes, stride=CAP * pieces), :] = placed[
                :, piece * LANES : (piece + 1) * LANES
            ]
    out_ref[...] = wide_ref[...].astype(BF16)


def total_kernel(ids_ref, message_ref, out_ref, wide_ref):
    nodes = ids_ref.shape[0]
    rows, width = out_ref.shape
    arrived = unpack(message_ref, wide_ref, nodes, width // LANES)
    ids = ids_ref[...]
    place = lax.broadcasted_iota(jnp.int32, (nodes, rows), 1)
    total = jnp.zeros((rows, width), F32)
    for slot in range(CAP):
        hot = jnp.where(ids[:, slot : slot + 1] == place, 1.0, 0.0).astype(BF16)
        total = total + dot(hot, arrived[slot], 0, 0)
    out_ref[...] = total.astype(BF16)


def kernel_call(body, out_shape, out_type, ins, wide=0, limit=32):
    return pl.pallas_call(
        body,
        out_shape=jax.ShapeDtypeStruct(out_shape, out_type),
        in_specs=ins,
        out_specs=VMEM,
        scratch_shapes=[pltpu.VMEM((wide, LANES), F32)] if wide else [],
        compiler_params=pltpu.CompilerParams(vmem_limit_bytes=limit << 20),
    )


def per_device(table, w_in, w_out, owner_node, item_row, history_lengths, cotangent):
    tokens = item_row.shape[0]
    nodes = lax.axis_size("node")
    locals_ = lax.axis_size("local")
    rows_here, width = table.shape
    pieces = width // LANES
    wide = nodes * CAP * pieces

    def exchange(message):
        message = message.reshape(nodes, CAP, pieces, LANES)
        message = lax.all_to_all(message, "node", split_axis=0, concat_axis=0, tiled=True)
        return message.reshape(wide, LANES)

    node_rows = lax.all_gather(table, "local", axis=0, tiled=True)
    sent = kernel_call(ask_kernel, (nodes, LANES), jnp.int32, [VMEM, VMEM])(
        owner_node, item_row.reshape(tokens, 1)
    )
    asked = lax.all_to_all(sent, "node", split_axis=0, concat_axis=0, tiled=True)
    answers = kernel_call(answer_kernel, (wide, LANES), BF16, [VMEM, VMEM], wide)(asked, node_rows)
    arrived = exchange(answers)
    grads = kernel_call(layer_kernel, (wide, LANES), BF16, [SMEM] + [VMEM] * 5, wide, 56)(
        history_lengths, owner_node, arrived, cotangent, w_in[0], w_out[0]
    )
    node_grads = exchange(grads)
    totals = kernel_call(total_kernel, (locals_ * rows_here, width), BF16, [VMEM, VMEM], wide)(
        asked, node_grads
    )
    totals = lax.all_to_all(
        totals.reshape(locals_, rows_here, width), "local", split_axis=0, concat_axis=0, tiled=True
    )
    return jnp.sum(totals.astype(F32), axis=0).astype(BF16)


def solution(mesh):
    return jax.shard_map(
        per_device,
        mesh=mesh,
        in_specs=(
            P(("node", "local"), None),
            P(),
            P(),
            P(("node", "local"), None),
            P(("node", "local")),
            P(("node", "local"), None),
            P(("node", "local"), None),
        ),
        out_specs=P(("node", "local"), None),
        check_vma=False,
    )
```

time: 223 us -> 161 us (0.72)
  the two profiles are of different devices: /device:TPU:1 before, /device:TPU:32 now
where the time goes in v1:
time: 161 us
  blocking collectives  131 us (81%)
  between operations  13.4 us (8%)
  Pallas kernels  9.85 us (6%)
  waiting for transfers between devices  3.07 us (2%)
  local copies, waits for them, and re-layouts  2.87 us (2%)
    all_to_all x2, blocking collectives, exchange(): lax.all_to_all(message, 'node', split_axis=0, concat_axis=0, tiled=True)  78.5 us
    all_to_all x1, blocking collectives, per_device(): lax.all_to_all(sent, 'node', split_axis=0, concat_axis=0, tiled=True)  33.4 us
    all_to_all x1, blocking collectives, per_device(): lax.all_to_all(totals.reshape(locals_, rows_here, width), 'local', split_...  18.9 us
    pallas_call x1, Pallas kernels, per_device(): kernel_call(layer_kernel, (wide, LANES), BF16, [SMEM] + [VMEM] * 5, wide,...  7.53 us
  transfers between devices with their start and end apart: 1, of which 1 were waited for; matrix products, arithmetic and copies ran while one was open for 1% of the time, Pallas kernels for 0%

profile of v1, /device:TPU:32, one launch (start us, length us, event | category | flops | bytes accessed | tf_op | source)
XLA Modules:
  0.0 160.9 jit_solution(2871576323374644965)
XLA Ops:
  6.5 0.0 all-gather.2.cloned.1.call-start
  6.5 0.7 all-gather.2.cloned.1.call-update
  7.3 0.8 copy.13.owner_ref
  8.1 0.0 copy-start
  8.1 0.8 copy.14.row_ref
  8.9 0.6 shard_map.73
  9.5 33.4 %all_to_all.26 = s32[128,1,128]{2,1,0:T(1,128)S(1)} all-to-all(s32[128,1,128]{2,1,0:T(1,128)S(1)} %bitcast.17), channel_id=1, replica_groups=mesh['node'=128,'local'=4] {'node'}, dimensions={0} | all-to-all | bytes 131072 | tf_op jit(solution)/shard_map/all_to_all | solution.py:210
  42.9 2.4 %all-gather.2.cloned.1.call-done.table_ref = bf16[1024,512]{1,0:T(8,128)(2,1)} async-done(((bf16[256,512]{1,0:T(8,128)(2,1)}), bf16[1024,512]{1,0:T(8,128)(2,1)}) %all-gather.2.cloned.1.call-update) | async-done | bytes 1048592 | tf_op jit(solution)/shard_map/all_gather | solution.py:206
  45.2 0.0 copy-start.1
  45.2 1.2 copy-done.1
  46.4 0.7 shard_map.74
  47.1 44.2 %all_to_all.27 = bf16[128,3,4,128]{3,2,1,0:T(4,128)(2,1)} all-to-all(bf16[128,3,4,128]{3,2,1,0:T(4,128)(2,1)S(1)} %bitcast.14), channel_id=1, replica_groups=mesh['node'=128,'local'=4] {'node'}, dimensions={0} | all-to-all | bytes 786432 | tf_op jit(solution)/shard_map/all_to_all | solution.py:203
  91.3 0.0 copy-done
  91.3 7.5 %shard_map.75 = bf16[1536,128]{1,0:T(8,128)(2,1)} custom-call(s32[1,4]{1,0:T(1,128)} %lengths_ref.1, s32[256,1]{1,0:T(8,128)} %copy-done, bf16[1536,128]{1,0:T(8,128)(2,1)} %bitcast.19, bf16[256,512]{1,0:T(8,128)(2,1)} %cot_ref.1, bf16[512,2048]{1,0:T(8,128)(2,1)} %bitcast.18, bf16[512,512]{1,0:T(8,128)(2,1)} %bitcast.21), custom_call_target="tpu_custom_call" | custom-call | tf_op jit(solution)/shard_map/pallas_call | solution.py:213
  98.8 34.4 %all_to_all.28 = bf16[128,3,4,128]{3,2,1,0:T(4,128)(2,1)S(1)} all-to-all(bf16[128,3,4,128]{3,2,1,0:T(4,128)(2,1)} %bitcast.20), channel_id=1, replica_groups=mesh['node'=128,'local'=4] {'node'}, dimensions={0} | all-to-all | bytes 786432 | tf_op jit(solution)/shard_map/all_to_all | solution.py:203
  133.2 1.1 shard_map.76
  134.3 18.9 %all_to_all.29 = bf16[4,256,512]{2,1,0:T(8,128)(2,1)S(1)} all-to-all(bf16[4,256,512]{2,1,0:T(8,128)(2,1)S(1)} %bitcast.12), channel_id=1, replica_groups=mesh['node'=128,'local'=4] {'local'}, dimensions={0} | all-to-all | bytes 2097152 | tf_op jit(solution)/shard_map/all_to_all | solution.py:220
  153.2 0.9 reduce_sum.12
Async XLA Ops:
  6.5 38.7 %all-gather.2.cloned.1.call-start = ((), (), s32[]{:S(2)}) async-start(), calls=%async_computation.4 | async-start | bytes 1310720 | tf_op jit(solution)/shard_map/all_gather | solution.py:206
  8.1 83.2 %copy-start = (s32[256,1]{1,0:T(8,128)}, s32[256,1]{1,0:T(8,128)S(1)}, u32[]{:S(2)}) copy-start(s32[256,1]{1,0:T(8,128)S(1)} %copy.13.owner_ref) | copy-start | bytes 3076
  45.2 1.2 copy-start.1
Sparse Core Ops, SparseCore 0:
  9.5 35.7 all-gather.1

commit v2 on v1

--- a/solution.py
+++ b/solution.py
@@ -21,45 +21,51 @@
 
 
 def ranked(owner, nodes):
-    count = owner.shape[0]
-    hot = owner == lax.broadcasted_iota(jnp.int32, (count, nodes), 1)
-    hot = jnp.where(hot, 1.0, 0.0)
+    count = owner.shape[1]
+    hot = jnp.where(owner == lax.broadcasted_iota(jnp.int32, (nodes, count), 0), 1.0, 0.0)
     row = lax.broadcasted_iota(jnp.int32, (count, count), 0)
     col = lax.broadcasted_iota(jnp.int32, (count, count), 1)
-    earlier = jnp.where(col < row, 1.0, 0.0).astype(BF16)
-    before = dot(earlier, hot.astype(BF16))
-    rank = jnp.sum(before * hot, axis=1, keepdims=True)
-    return hot, rank
+    earlier = jnp.where(row < col, 1.0, 0.0).astype(BF16)
+    before = dot(hot.astype(BF16), earlier)
+    return hot, jnp.sum(before * hot, axis=0, keepdims=True)
 
 
 def ask_kernel(owner_ref, row_ref, ids_ref):
-    nodes = ids_ref.shape[0]
-    count = owner_ref.shape[0]
+    nodes, lanes = ids_ref.shape
+    count = owner_ref.shape[1]
     hot, rank = ranked(owner_ref[...], nodes)
     rows = row_ref[...]
-    place = lax.broadcasted_iota(jnp.int32, (count, LANES), 1) == rank.astype(jnp.int32)
+    place = lax.broadcasted_iota(jnp.int32, (lanes, count), 0) == rank.astype(jnp.int32)
     high = jnp.where(place, (rows >> 5).astype(F32), 0.0).astype(BF16)
     low = jnp.where(place, (rows & 31).astype(F32), 0.0).astype(BF16)
     hot = hot.astype(BF16)
-    ids = dot(hot, high, 0, 0) * 32.0 + dot(hot, low, 0, 0)
+    ids = dot(hot, high, 1, 1) * 32.0 + dot(hot, low, 1, 1)
     ids_ref[...] = ids.astype(jnp.int32)
 
 
-def answer_kernel(ids_ref, table_ref, out_ref, wide_ref):
+def answer_kernel(place_ref, ids_ref, *refs):
+    blocks, out_ref, wide_ref = refs[:-2], refs[-2], refs[-1]
     nodes = ids_ref.shape[0]
-    rows, width = table_ref.shape
+    rows, width = blocks[0].shape
     pieces = width // LANES
-    ids = ids_ref[...]
-    table = table_ref[...]
-    place = lax.broadcasted_iota(jnp.int32, (nodes, rows), 1)
-    for slot in range(CAP):
-        hot = jnp.where(ids[:, slot : slot + 1] == place, 1.0, 0.0).astype(BF16)
-        picked = dot(hot, table)
-        for piece in range(pieces):
-            wide_ref[pl.ds(slot * pieces + piece, nodes, stride=CAP * pieces), :] = picked[
-                :, piece * LANES : (piece + 1) * LANES
-            ]
+    ids = ids_ref[...] - place_ref[0] * rows
+    ids = jnp.where(ids < 0, ids + len(blocks) * rows, ids)
+    at = lax.broadcasted_iota(jnp.int32, (nodes, rows), 1)
+    tables = [block[...] for block in blocks]
+    for slot in range(CAP):
+        picked = jnp.zeros((nodes, width), F32)
+        for turn, table in enumerate(tables):
+            hot = jnp.where(ids[:, slot : slot + 1] - turn * rows == at, 1.0, 0.0).astype(BF16)
+            picked = picked + dot(hot, table)
+        spread(picked, slot, wide_ref, nodes, pieces)
     out_ref[...] = wide_ref[...].astype(BF16)
+
+
+def spread(value, slot, wide_ref, nodes, pieces):
+    for piece in range(pieces):
+        wide_ref[pl.ds(slot * pieces + piece, nodes, stride=CAP * pieces), :] = value[
+            :, piece * LANES : (piece + 1) * LANES
+        ]
 
 
 def unpack(message_ref, wide_ref, nodes, pieces):
@@ -104,7 +110,7 @@
     hot, rank = ranked(owner_ref[...], nodes)
     picks = [jnp.where(rank == float(slot), hot, 0.0).astype(BF16) for slot in range(CAP)]
     arrived = unpack(message_ref, wide_ref, nodes, pieces)
-    embedded = dot(jnp.concatenate(picks, axis=1), jnp.concatenate(arrived, axis=0))
+    embedded = dot(jnp.concatenate(picks, axis=0), jnp.concatenate(arrived, axis=0), 0, 0)
 
     row = lax.broadcasted_iota(jnp.int32, (tokens, 1), 0)
     col = lax.broadcasted_iota(jnp.int32, (1, tokens), 1)
@@ -158,11 +164,7 @@
     grads = cot.astype(F32) + centre_back(normed, inverse, normed_cot.astype(BF16).astype(F32))
     grads = grads.astype(BF16)
     for slot in range(CAP):
-        placed = dot(picks[slot], grads, 0, 0)
-        for piece in range(pieces):
-            wide_ref[pl.ds(slot * pieces + piece, nodes, stride=CAP * pieces), :] = placed[
-                :, piece * LANES : (piece + 1) * LANES
-            ]
+        spread(dot(picks[slot], grads), slot, wide_ref, nodes, pieces)
     out_ref[...] = wide_ref[...].astype(BF16)
 
 
@@ -176,6 +178,13 @@
     for slot in range(CAP):
         hot = jnp.where(ids[:, slot : slot + 1] == place, 1.0, 0.0).astype(BF16)
         total = total + dot(hot, arrived[slot], 0, 0)
+    out_ref[...] = total.astype(BF16)
+
+
+def sum_kernel(parts_ref, out_ref):
+    total = parts_ref[0].astype(F32)
+    for part in range(1, parts_ref.shape[0]):
+        total = total + parts_ref[part].astype(F32)
     out_ref[...] = total.astype(BF16)
 
 
@@ -203,15 +212,22 @@
         message = lax.all_to_all(message, "node", split_axis=0, concat_axis=0, tiled=True)
         return message.reshape(wide, LANES)
 
-    node_rows = lax.all_gather(table, "local", axis=0, tiled=True)
+    def turned(block, by):
+        return lax.ppermute(block, "local", [((i + by) % locals_, i) for i in range(locals_)])
+
+    blocks = [table] + [turned(table, by) for by in range(1, locals_)]
+    owner = owner_node.reshape(1, tokens)
     sent = kernel_call(ask_kernel, (nodes, LANES), jnp.int32, [VMEM, VMEM])(
-        owner_node, item_row.reshape(tokens, 1)
+        owner, item_row.reshape(1, tokens)
     )
     asked = lax.all_to_all(sent, "node", split_axis=0, concat_axis=0, tiled=True)
-    answers = kernel_call(answer_kernel, (wide, LANES), BF16, [VMEM, VMEM], wide)(asked, node_rows)
+    place = lax.axis_index("local").reshape(1)
+    answers = kernel_call(
+        answer_kernel, (wide, LANES), BF16, [SMEM, VMEM] + [VMEM] * locals_, wide
+    )(place, asked, *blocks)
     arrived = exchange(answers)
     grads = kernel_call(layer_kernel, (wide, LANES), BF16, [SMEM] + [VMEM] * 5, wide, 56)(
-        history_lengths, owner_node, arrived, cotangent, w_in[0], w_out[0]
+        history_lengths, owner, arrived, cotangent, w_in[0], w_out[0]
     )
     node_grads = exchange(grads)
     totals = kernel_call(total_kernel, (locals_ * rows_here, width), BF16, [VMEM, VMEM], wide)(
@@ -220,7 +236,7 @@
     totals = lax.all_to_all(
         totals.reshape(locals_, rows_here, width), "local", split_axis=0, concat_axis=0, tiled=True
     )
-    return jnp.sum(totals.astype(F32), axis=0).astype(BF16)
+    return kernel_call(sum_kernel, (rows_here, width), BF16, [VMEM])(totals)
 
 
 def solution(mesh):

time: 161 us -> 146 us (0.907)
  blocking collectives: 131 us -> 87.8 us
  starting transfers between devices: 0.01 us -> 29.9 us
  between operations: 13.4 us -> 0.08 us
  waiting for transfers between devices: 3.07 us -> 14.3 us
    all_to_all x1 -> x0, blocking collectives: 33.4 us -> none  [per_device(): lax.all_to_all(sent, 'node', split_axis=0, concat_axis=0, tiled=True)]
    all_to_all x0 -> x1, starting transfers between devices: none -> 19.2 us  [per_device(): lax.all_to_all(sent, 'node', split_axis=0, concat_axis=0, tiled=True)]
    all_to_all x0 -> x1, waiting for transfers between devices: none -> 14.3 us  [per_device(): lax.all_to_all(sent, 'node', split_axis=0, concat_axis=0, tiled=True)]
    ppermute x0 -> x3, starting transfers between devices: none -> 10.8 us  [turned(): lax.ppermute(block, 'local', [((i + by) % locals_, i) for i in range(loca...]
    all_to_all x2, blocking collectives: 78.5 us -> 68.6 us  [exchange(): lax.all_to_all(message, 'node', split_axis=0, concat_axis=0, tiled=True)]
    all_gather x1 -> x0, waiting for transfers between devices: 2.36 us -> none  [per_device(): node_rows = lax.all_gather(table, 'local', axis=0, tiled=True)]
  transfers between devices with their start and end apart: 1 -> 4, of which waited for: 1 -> 1; matrix products, arithmetic and copies ran while one was open for 1% -> 0% of each run, Pallas kernels for 0% -> 1%
where the time goes in v2:
time: 146 us; the launch traced here: 145 us
  blocking collectives  87.8 us (60%)
  starting transfers between devices  29.9 us (20%)
  waiting for transfers between devices  14.3 us (10%)
  Pallas kernels  11.1 us (8%)
  local copies, waits for them, and re-layouts  2.3 us (2%)
    all_to_all x2, blocking collectives, exchange(): lax.all_to_all(message, 'node', split_axis=0, concat_axis=0, tiled=True)  68.6 us
    all_to_all x1, blocking collectives, per_device(): lax.all_to_all(totals.reshape(locals_, rows_here, width), 'local', split_...  19.2 us
    all_to_all x1, starting transfers between devices, per_device(): lax.all_to_all(sent, 'node', split_axis=0, concat_axis=0, tiled=True)  19.2 us
    all_to_all x1, waiting for transfers between devices, per_device(): lax.all_to_all(sent, 'node', split_axis=0, concat_axis=0, tiled=True)  14.3 us
    ppermute x3, starting transfers between devices, turned(): lax.ppermute(block, 'local', [((i + by) % locals_, i) for i in range(loca...  10.8 us
    pallas_call x1, Pallas kernels, per_device(): kernel_call(layer_kernel, (wide, LANES), BF16, [SMEM] + [VMEM] * 5, wide,...  7.45 us
  transfers between devices with their start and end apart: 4, of which 1 were waited for; matrix products, arithmetic and copies ran while one was open for 0% of the time, Pallas kernels for 1%

profile of v2, /device:TPU:32, one launch (start us, length us, event | category | flops | bytes accessed | tf_op | source)
XLA Modules:
  0.0 145.5 jit_solution(1490872041912699392)
XLA Ops:
  0.0 4.9 %collective-permute-start.1 = (bf16[256,512]{1,0:T(8,128)(2,1)}, bf16[256,512]{1,0:T(8,128)(2,1)S(1)}, u32[]{:S(2)}, u32[]{:S(2)}) collective-permute-start(bf16[256,512]{1,0:T(8,128)(2,1)} %refs_0_.1), channel_id=1, source_target_pairs={{2,0},{3,1},{0,2},{1,3},{6,4},{7,5},{4,6},{5,7},{10,8},{11,9},{8,1... | collective-permute-start | bytes 786440 | tf_op jit(solution)/shard_map/ppermute | solution.py:216
  4.9 3.1 %collective-permute-start = (bf16[256,512]{1,0:T(8,128)(2,1)}, bf16[256,512]{1,0:T(8,128)(2,1)S(1)}, u32[]{:S(2)}, u32[]{:S(2)}) collective-permute-start(bf16[256,512]{1,0:T(8,128)(2,1)} %refs_0_.1), channel_id=1, source_target_pairs={{1,0},{2,1},{3,2},{0,3},{5,4},{6,5},{7,6},{4,7},{9,8},{10,9},{11,1... | collective-permute-start | bytes 786440 | tf_op jit(solution)/shard_map/ppermute | solution.py:216
  8.0 2.8 %collective-permute-start.2 = (bf16[256,512]{1,0:T(8,128)(2,1)}, bf16[256,512]{1,0:T(8,128)(2,1)S(1)}, u32[]{:S(2)}, u32[]{:S(2)}) collective-permute-start(bf16[256,512]{1,0:T(8,128)(2,1)} %refs_0_.1), channel_id=1, source_target_pairs={{3,0},{0,1},{1,2},{2,3},{7,4},{4,5},{5,6},{6,7},{11,8},{8,9},{9,10... | collective-permute-start | bytes 786440 | tf_op jit(solution)/shard_map/ppermute | solution.py:216
  10.8 0.0 copy-start.1
  10.8 0.7 copy-done.1
  11.5 0.0 copy-start.2
  11.5 0.7 copy-done.2
  12.2 1.0 shard_map.73
  13.2 19.2 %all-to-all-start = ((s32[128,1,128]{2,1,0:T(1,128)}), s32[128,1,128]{2,1,0:T(1,128)S(1)}, u32[]{:S(2)}, u32[]{:S(2)}) async-start(s32[128,1,128]{2,1,0:T(1,128)} %bitcast.3), calls=%async_computation | async-start | bytes 131072 | tf_op jit(solution)/shard_map/all_to_all | solution.py:223
  32.4 14.3 %all-to-all-done = s32[128,1,128]{2,1,0:T(1,128)S(1)} async-done(((s32[128,1,128]{2,1,0:T(1,128)}), s32[128,1,128]{2,1,0:T(1,128)S(1)}, u32[]{:S(2)}, u32[]{:S(2)}) %all-to-all-start) | async-done | bytes 65568 | tf_op jit(solution)/shard_map/all_to_all | solution.py:223
  46.7 0.0 collective-permute-done.1.refs_2_
  46.7 0.0 collective-permute-done.refs_1_
  46.7 0.0 collective-permute-done.2.refs_3_
  46.7 0.0 copy-start
  46.7 0.9 copy-done
  47.7 0.7 shard_map.74
  48.3 34.2 %all_to_all.26 = bf16[128,3,4,128]{3,2,1,0:T(4,128)(2,1)} all-to-all(bf16[128,3,4,128]{3,2,1,0:T(4,128)(2,1)S(1)} %bitcast.15), channel_id=1, replica_groups=mesh['node'=128,'local'=4] {'node'}, dimensions={0} | all-to-all | bytes 786432 | tf_op jit(solution)/shard_map/all_to_all | solution.py:212
  82.5 7.4 %shard_map.75 = bf16[1536,128]{1,0:T(8,128)(2,1)} custom-call(s32[1,4]{1,0:T(1,128)} %lengths_ref.1, s32[1,256]{1,0:T(1,128)} %bitcast.19, bf16[1536,128]{1,0:T(8,128)(2,1)} %bitcast.23, bf16[256,512]{1,0:T(8,128)(2,1)} %cot_ref.1, bf16[512,2048]{1,0:T(8,128)(2,1)} %bitcast.22, bf16[512,512]{1,0:T(8,128)(2,1)} %bitcast.25), custom_call_target="tpu_custom_call" | custom-call | tf_op jit(solution)/shard_map/pallas_call | solution.py:229
  90.0 34.4 %all_to_all.27 = bf16[128,3,4,128]{3,2,1,0:T(4,128)(2,1)S(1)} all-to-all(bf16[128,3,4,128]{3,2,1,0:T(4,128)(2,1)} %bitcast.24), channel_id=1, replica_groups=mesh['node'=128,'local'=4] {'node'}, dimensions={0} | all-to-all | bytes 786432 | tf_op jit(solution)/shard_map/all_to_all | solution.py:212
  124.4 1.1 shard_map.76
  125.4 19.2 %all_to_all.28.parts_ref = bf16[4,256,512]{2,1,0:T(8,128)(2,1)S(1)} all-to-all(bf16[4,256,512]{2,1,0:T(8,128)(2,1)S(1)} %bitcast.14), channel_id=1, replica_groups=mesh['node'=128,'local'=4] {'local'}, dimensions={0} | all-to-all | bytes 2097152 | tf_op jit(solution)/shard_map/all_to_all | solution.py:236
  144.6 0.8 shard_map.77
Async XLA Ops:
  0.0 46.7 %collective-permute-start.1 = (bf16[256,512]{1,0:T(8,128)(2,1)}, bf16[256,512]{1,0:T(8,128)(2,1)S(1)}, u32[]{:S(2)}, u32[]{:S(2)}) collective-permute-start(bf16[256,512]{1,0:T(8,128)(2,1)} %refs_0_.1), channel_id=1, source_target_pairs={{2,0},{3,1},{0,2},{1,3},{6,4},{7,5},{4,6},{5,7},{10,8},{11,9},{8,1... | collective-permute-start | bytes 786440 | tf_op jit(solution)/shard_map/ppermute | solution.py:216
  4.9 41.8 %collective-permute-start = (bf16[256,512]{1,0:T(8,128)(2,1)}, bf16[256,512]{1,0:T(8,128)(2,1)S(1)}, u32[]{:S(2)}, u32[]{:S(2)}) collective-permute-start(bf16[256,512]{1,0:T(8,128)(2,1)} %refs_0_.1), channel_id=1, source_target_pairs={{1,0},{2,1},{3,2},{0,3},{5,4},{6,5},{7,6},{4,7},{9,8},{10,9},{11,1... | collective-permute-start | bytes 786440 | tf_op jit(solution)/shard_map/ppermute | solution.py:216
  8.0 38.7 %collective-permute-start.2 = (bf16[256,512]{1,0:T(8,128)(2,1)}, bf16[256,512]{1,0:T(8,128)(2,1)S(1)}, u32[]{:S(2)}, u32[]{:S(2)}) collective-permute-start(bf16[256,512]{1,0:T(8,128)(2,1)} %refs_0_.1), channel_id=1, source_target_pairs={{3,0},{0,1},{1,2},{2,3},{7,4},{4,5},{5,6},{6,7},{11,8},{8,9},{9,10... | collective-permute-start | bytes 786440 | tf_op jit(solution)/shard_map/ppermute | solution.py:216
  10.8 0.7 copy-start.1
  11.5 0.7 copy-start.2
  13.2 33.5 %all-to-all-start = ((s32[128,1,128]{2,1,0:T(1,128)}), s32[128,1,128]{2,1,0:T(1,128)S(1)}, u32[]{:S(2)}, u32[]{:S(2)}) async-start(s32[128,1,128]{2,1,0:T(1,128)} %bitcast.3), calls=%async_computation | async-start | bytes 131072 | tf_op jit(solution)/shard_map/all_to_all | solution.py:223
  46.7 1.0 copy-start

commit v3 on v2

--- a/solution.py
+++ b/solution.py
@@ -134,14 +134,16 @@
         slopes.append(slope)
     gate_rows, value_rows, query_rows, key_rows = parts
     scale = 1.0 / math.sqrt(head)
+    weights = weights * scale
     attentions, score_slopes, mixed = [], [], []
     for e in range(HEADS):
         cols = slice(e * head, (e + 1) * head)
-        kept, slope = gated(dot(query_rows[:, cols], key_rows[:, cols], 1, 1) * scale)
-        attention = (kept * weights).astype(BF16)
-        attentions.append(attention)
-        score_slopes.append(slope * (weights * scale))
-        mixed.append(dot(attention, value_rows[:, cols]))
+        scores = dot(query_rows[:, cols], key_rows[:, cols], 1, 1)
+        gate = 0.5 + 0.5 * jnp.tanh((0.5 * scale) * scores)
+        kept = scores * gate * weights
+        score_slopes.append(weights * gate + kept * (scale - scale * gate))
+        attentions.append(kept.astype(BF16))
+        mixed.append(dot(attentions[e], value_rows[:, cols]))
     mixed_normed, mixed_inverse = centre(jnp.concatenate(mixed, axis=1))
 
     cot = cot_ref[...]
@@ -199,6 +201,10 @@
     )
 
 
+def layer_call(wide, limit=24):
+    return kernel_call(layer_kernel, (wide, LANES), BF16, [SMEM] + [VMEM] * 5, wide, limit)
+
+
 def per_device(table, w_in, w_out, owner_node, item_row, history_lengths, cotangent):
     tokens = item_row.shape[0]
     nodes = lax.axis_size("node")
@@ -217,7 +223,7 @@
 
     blocks = [table] + [turned(table, by) for by in range(1, locals_)]
     owner = owner_node.reshape(1, tokens)
-    sent = kernel_call(ask_kernel, (nodes, LANES), jnp.int32, [VMEM, VMEM])(
+    sent = kernel_call(ask_kernel, (nodes, LANES), jnp.int32, [VMEM, VMEM], limit=60)(
         owner, item_row.reshape(1, tokens)
     )
     asked = lax.all_to_all(sent, "node", split_axis=0, concat_axis=0, tiled=True)
@@ -226,7 +232,7 @@
         answer_kernel, (wide, LANES), BF16, [SMEM, VMEM] + [VMEM] * locals_, wide
     )(place, asked, *blocks)
     arrived = exchange(answers)
-    grads = kernel_call(layer_kernel, (wide, LANES), BF16, [SMEM] + [VMEM] * 5, wide, 56)(
+    grads = layer_call(wide)(
         history_lengths, owner, arrived, cotangent, w_in[0], w_out[0]
     )
     node_grads = exchange(grads)

time: 146 us -> 143 us (0.979)
  Pallas kernels: 11.1 us -> 9.51 us
    pallas_call x2, Pallas kernels: 8.48 us -> 6.94 us  [the longest x1 5.21 us: per_device(): layer_call(wide)]
where the time goes in v3:
time: 143 us
  blocking collectives  87 us (61%)
  starting transfers between devices  30.1 us (21%)
  waiting for transfers between devices  14.3 us (10%)
  Pallas kernels  9.51 us (7%)
  local copies, waits for them, and re-layouts  2 us (1%)
    all_to_all x2, blocking collectives, exchange(): lax.all_to_all(message, 'node', split_axis=0, concat_axis=0, tiled=True)  67.9 us
    all_to_all x1, blocking collectives, per_device(): lax.all_to_all(totals.reshape(locals_, rows_here, width), 'local', split_...  19.2 us
    all_to_all x1, starting transfers between devices, per_device(): lax.all_to_all(sent, 'node', split_axis=0, concat_axis=0, tiled=True)  19.2 us
    all_to_all x1, waiting for transfers between devices, per_device(): lax.all_to_all(sent, 'node', split_axis=0, concat_axis=0, tiled=True)  14.3 us
    ppermute x3, starting transfers between devices, turned(): lax.ppermute(block, 'local', [((i + by) % locals_, i) for i in range(loca...  10.9 us
    pallas_call x1, Pallas kernels, per_device(): layer_call(wide)  5.21 us
  transfers between devices with their start and end apart: 4, of which 1 were waited for; matrix products, arithmetic and copies ran while one was open for 0% of the time, Pallas kernels for 1%

profile of v3, /device:TPU:32, one launch (start us, length us, event | category | flops | bytes accessed | tf_op | source)
XLA Modules:
  0.0 143.0 jit_solution(4288564562323214591)
XLA Ops:
  0.0 0.0 copy-start.2
  0.0 0.0 copy-start
  0.0 5.1 %collective-permute-start.1 = (bf16[256,512]{1,0:T(8,128)(2,1)}, bf16[256,512]{1,0:T(8,128)(2,1)S(1)}, u32[]{:S(2)}, u32[]{:S(2)}) collective-permute-start(bf16[256,512]{1,0:T(8,128)(2,1)} %refs_0_.1), channel_id=1, source_target_pairs={{2,0},{3,1},{0,2},{1,3},{6,4},{7,5},{4,6},{5,7},{10,8},{11,9},{8,1... | collective-permute-start | bytes 786440 | tf_op jit(solution)/shard_map/ppermute | solution.py:222
  5.1 3.1 %collective-permute-start = (bf16[256,512]{1,0:T(8,128)(2,1)}, bf16[256,512]{1,0:T(8,128)(2,1)S(1)}, u32[]{:S(2)}, u32[]{:S(2)}) collective-permute-start(bf16[256,512]{1,0:T(8,128)(2,1)} %refs_0_.1), channel_id=1, source_target_pairs={{1,0},{2,1},{3,2},{0,3},{5,4},{6,5},{7,6},{4,7},{9,8},{10,9},{11,1... | collective-permute-start | bytes 786440 | tf_op jit(solution)/shard_map/ppermute | solution.py:222
  8.1 2.8 %collective-permute-start.2 = (bf16[256,512]{1,0:T(8,128)(2,1)}, bf16[256,512]{1,0:T(8,128)(2,1)S(1)}, u32[]{:S(2)}, u32[]{:S(2)}) collective-permute-start(bf16[256,512]{1,0:T(8,128)(2,1)} %refs_0_.1), channel_id=1, source_target_pairs={{3,0},{0,1},{1,2},{2,3},{7,4},{4,5},{5,6},{6,7},{11,8},{8,9},{9,10... | collective-permute-start | bytes 786440 | tf_op jit(solution)/shard_map/ppermute | solution.py:222
  10.9 1.7 %shard_map.73 = s32[128,128]{1,0:T(8,128)} custom-call(s32[1,256]{1,0:T(1,128)} %bitcast.23, s32[1,256]{1,0:T(1,128)} %bitcast.26), custom_call_target="tpu_custom_call" | custom-call | tf_op jit(solution)/shard_map/pallas_call | solution.py:226
  12.7 19.2 %all-to-all-start = ((s32[128,1,128]{2,1,0:T(1,128)}), s32[128,1,128]{2,1,0:T(1,128)S(1)}, u32[]{:S(2)}, u32[]{:S(2)}) async-start(s32[128,1,128]{2,1,0:T(1,128)} %bitcast.25), calls=%async_computation | async-start | bytes 131072 | tf_op jit(solution)/shard_map/all_to_all | solution.py:229
  31.8 14.3 %all-to-all-done = s32[128,1,128]{2,1,0:T(1,128)S(1)} async-done(((s32[128,1,128]{2,1,0:T(1,128)}), s32[128,1,128]{2,1,0:T(1,128)S(1)}, u32[]{:S(2)}, u32[]{:S(2)}) %all-to-all-start) | async-done | bytes 65568 | tf_op jit(solution)/shard_map/all_to_all | solution.py:229
  46.2 0.0 collective-permute-done.1.refs_2_
  46.2 0.0 collective-permute-done.refs_1_
  46.2 0.0 collective-permute-done.2.refs_3_
  46.2 0.0 copy-start.3
  46.2 0.9 copy-done.3
  47.1 0.0 copy-start.4
  47.1 0.0 copy-start.5
  47.1 0.7 shard_map.74
  47.8 33.7 %all_to_all.26 = bf16[128,3,4,128]{3,2,1,0:T(4,128)(2,1)S(1)} all-to-all(bf16[128,3,4,128]{3,2,1,0:T(4,128)(2,1)S(1)} %bitcast.16), channel_id=1, replica_groups=mesh['node'=128,'local'=4] {'node'}, dimensions={0} | all-to-all | bytes 786432 | tf_op jit(solution)/shard_map/all_to_all | solution.py:218
  81.5 0.0 copy-done.2
  81.5 0.0 copy-done
  81.5 0.0 copy-done.4
  81.5 0.0 copy-done.5
  81.5 0.0 copy-start.1
  81.5 1.0 copy-done.1
  82.5 5.2 %shard_map.75 = bf16[1536,128]{1,0:T(8,128)(2,1)S(1)} custom-call(s32[1,4]{1,0:T(1,128)S(1)} %copy-done.5, s32[1,256]{1,0:T(1,128)S(1)} %bitcast.24, bf16[1536,128]{1,0:T(8,128)(2,1)S(1)} %bitcast.18, bf16[256,512]{1,0:T(8,128)(2,1)S(1)} %copy-done.2, bf16[512,2048]{1,0:T(8,128)(2,1)S(1)} %bitcast.15, bf16[512,512]{1,0:T(8,128)(2,1)S(1)} %bitcast.22), custom_call_target="tpu_custom_call" | custom-call | tf_op jit(solution)/shard_map/pallas_call | solution.py:235
  87.8 34.2 %all_to_all.27 = bf16[128,3,4,128]{3,2,1,0:T(4,128)(2,1)S(1)} all-to-all(bf16[128,3,4,128]{3,2,1,0:T(4,128)(2,1)S(1)} %bitcast.19), channel_id=1, replica_groups=mesh['node'=128,'local'=4] {'node'}, dimensions={0} | all-to-all | bytes 786432 | tf_op jit(solution)/shard_map/all_to_all | solution.py:218
  121.9 1.1 shard_map.76
  123.0 19.2 %all_to_all.28.parts_ref = bf16[4,256,512]{2,1,0:T(8,128)(2,1)S(1)} all-to-all(bf16[4,256,512]{2,1,0:T(8,128)(2,1)S(1)} %bitcast.14), channel_id=1, replica_groups=mesh['node'=128,'local'=4] {'local'}, dimensions={0} | all-to-all | bytes 2097152 | tf_op jit(solution)/shard_map/all_to_all | solution.py:242
  142.2 0.8 shard_map.77
Async XLA Ops:
  0.0 81.5 %copy-start.2 = (bf16[256,512]{1,0:T(8,128)(2,1)S(1)}, bf16[256,512]{1,0:T(8,128)(2,1)}, u32[]{:S(2)}) copy-start(bf16[256,512]{1,0:T(8,128)(2,1)} %cot_ref.1) | copy-start | bytes 786436
  0.0 81.5 %copy-start = (bf16[1,512,2048]{2,1,0:T(8,128)(2,1)S(1)}, bf16[1,512,2048]{2,1,0:T(8,128)(2,1)}, u32[]{:S(2)}) copy-start(bf16[1,512,2048]{2,1,0:T(8,128)(2,1)} %param.8) | copy-start | bytes 6291460
  0.0 46.2 %collective-permute-start.1 = (bf16[256,512]{1,0:T(8,128)(2,1)}, bf16[256,512]{1,0:T(8,128)(2,1)S(1)}, u32[]{:S(2)}, u32[]{:S(2)}) collective-permute-start(bf16[256,512]{1,0:T(8,128)(2,1)} %refs_0_.1), channel_id=1, source_target_pairs={{2,0},{3,1},{0,2},{1,3},{6,4},{7,5},{4,6},{5,7},{10,8},{11,9},{8,1... | collective-permute-start | bytes 786440 | tf_op jit(solution)/shard_map/ppermute | solution.py:222
  5.1 41.1 %collective-permute-start = (bf16[256,512]{1,0:T(8,128)(2,1)}, bf16[256,512]{1,0:T(8,128)(2,1)S(1)}, u32[]{:S(2)}, u32[]{:S(2)}) collective-permute-start(bf16[256,512]{1,0:T(8,128)(2,1)} %refs_0_.1), channel_id=1, source_target_pairs={{1,0},{2,1},{3,2},{0,3},{5,4},{6,5},{7,6},{4,7},{9,8},{10,9},{11,1... | collective-permute-start | bytes 786440 | tf_op jit(solution)/shard_map/ppermute | solution.py:222
  8.1 38.0 %collective-permute-start.2 = (bf16[256,512]{1,0:T(8,128)(2,1)}, bf16[256,512]{1,0:T(8,128)(2,1)S(1)}, u32[]{:S(2)}, u32[]{:S(2)}) collective-permute-start(bf16[256,512]{1,0:T(8,128)(2,1)} %refs_0_.1), channel_id=1, source_target_pairs={{3,0},{0,1},{1,2},{2,3},{7,4},{4,5},{5,6},{6,7},{11,8},{8,9},{9,10... | collective-permute-start | bytes 786440 | tf_op jit(solution)/shard_map/ppermute | solution.py:222
  12.7 33.5 %all-to-all-start = ((s32[128,1,128]{2,1,0:T(1,128)}), s32[128,1,128]{2,1,0:T(1,128)S(1)}, u32[]{:S(2)}, u32[]{:S(2)}) async-start(s32[128,1,128]{2,1,0:T(1,128)} %bitcast.25), calls=%async_computation | async-start | bytes 131072 | tf_op jit(solution)/shard_map/all_to_all | solution.py:229
  46.2 1.0 copy-start.3
  47.1 34.4 %copy-start.4 = (s32[256,1]{0,1:T(1,128)S(1)}, s32[256,1]{0,1:T(1,128)}, u32[]{:S(2)}) copy-start(s32[256,1]{0,1:T(1,128)} %param.10) | copy-start | bytes 3076
  47.1 34.4 %copy-start.5 = (s32[1,4]{1,0:T(1,128)S(1)}, s32[1,4]{1,0:T(1,128)}, u32[]{:S(2)}) copy-start(s32[1,4]{1,0:T(1,128)} %lengths_ref.1) | copy-start | bytes 52
  81.5 1.0 copy-start.1
